TPU v7x, 512 devices: a whole 4x8x8 slice. The times are simulated.
512 devices in a mesh: row: 16 (over z, y_hi), col: 32 (over x, y_lo, core).
Axes of the slice: x: 4, y: 8 (y_hi: 2, y_lo: 4; y = y_hi * 4 + y_lo), z: 8, core: 2. Of those that a mesh axis runs over, the one named last changes fastest.
Arguments:
- tokens: bfloat16 [384, 12288], P('col', 'row'), may hold values from -6 to 6
- up_weight: bfloat16 [12288, 49152], P('row', 'col'), may hold values from -0.0546875 to 0.0546875
- up_bias: float32 [49152], P('col'), may hold values from -3 to 3
- down_weight: bfloat16 [49152, 12288], P('col', 'row'), may hold values from -0.02734375 to 0.02734375
- down_bias: float32 [12288], P('row'), may hold values from -3 to 3
Outputs:
- layer_out: bfloat16 [384, 12288], P('col', 'row')
All inputs are finite; a program needn't handle non-finite values.
Results may differ from a plain program's by a relative error of at most 0.0034.
Values may be sent and summed in bfloat16 or wider, within the bound.
No kernel may reach another device: no remote copies, remote signals or barrier semaphores. Data moves between devices by JAX's collectives and lax.ppermute only.
A program may use at most 64 MiB of HBM per device.

v0:
```python
import jax
import jax.numpy as jnp
from jax import lax
from jax.sharding import PartitionSpec as P


def on_device(tokens, up_weight, up_bias, down_weight, down_bias):
    gathered = lax.all_gather(tokens, "col", axis=0, tiled=True)
    partial_up = jnp.dot(gathered, up_weight, preferred_element_type=jnp.float32)
    summed_up = lax.psum(partial_up, "row")
    activated = jax.nn.gelu(summed_up + up_bias, approximate=True).astype(jnp.bfloat16)
    branch = lax.psum_scatter(
        jnp.dot(activated, down_weight, preferred_element_type=jnp.float32),
        "col",
        scatter_dimension=0,
        tiled=True,
    )
    return (tokens.astype(jnp.float32) + branch + down_bias).astype(jnp.bfloat16)


def solution(mesh):
    placed = (P("col", "row"), P("row", "col"), P("col"), P("col", "row"), P("row"))
    return jax.shard_map(
        on_device, mesh=mesh, in_specs=placed, out_specs=P("col", "row"), check_vma=False
    )
```

profile of v0, /device:TPU:1, one launch (start us, length us, event | category | flops | bytes accessed | tf_op | source)
XLA Modules:
  0.0 432.2 jit_solution(3478070674415503731)
XLA Ops:
  6.5 0.0 copy-start
  6.5 0.0 all-reduce.4.cloned.1.call-start
  6.5 48.6 %all-gather = bf16[32,12,768]{2,1,0:T(8,128)(2,1)S(1)} all-gather(bf16[1,12,768]{2,1,0:T(8,128)(2,1)} %bitcast.7), channel_id=1, replica_groups=mesh['row'=16,'col'=32] {'col'}, dimensions={0}, use_global_device_ids=true | all-gather | bytes 608256 | tf_op jit(solution)/shard_map/all_gather | solution.py:8
  55.1 1.0 reshape.3
  56.1 0.0 copy-done
  56.1 3.6 fusion.17
  59.7 0.0 copy-start.2
  59.7 0.0 all-reduce.4.cloned.1.call-update
  59.7 0.0 copy-start.1
  59.7 251.4 %all-reduce.4.cloned.1.call-done = f32[384,1536]{1,0:T(8,128)} async-done(((f32[384,1536]{1,0:T(8,128)}), f32[384,1536]{1,0:T(8,128)}) %all-reduce.4.cloned.1.call-update) | async-done | bytes 2359312 | tf_op jit(solution)/shard_map/psum | solution.py:10
  311.1 0.0 copy-done.2
  311.1 4.0 fusion.9
  315.0 82.6 %fusion = f32[16,768]{1,0:T(8,128)} fusion(f32[384,768]{1,0:T(8,128)S(1)} %fusion.9), kind=kCustom, calls=%all-reduce-scatter | all-reduce-scatter fusion | flops 393217 | bytes 1230848
  397.6 1.9 collective-permute-start
  399.6 1.3 collective-permute-start.1
  400.9 0.8 slice
  401.7 1.3 collective-permute-start.7
  403.0 1.3 collective-permute-start.2
  404.3 1.4 collective-permute-start.3
  405.6 0.0 collective-permute-done.7
  405.6 4.6 %collective-permute-start.4 = (f32[16,768]{1,0:T(8,128)}, f32[16,768]{1,0:T(8,128)S(1)}, u32[]{:S(2)}, u32[]{:S(2)}) collective-permute-start(f32[16,768]{1,0:T(8,128)} %fusion), channel_id=1, source_target_pairs={{0,5},{1,6},{2,7},{3,8},{4,9},{5,10},{6,11},{7,12},{8,13},{9,14},{... | collective-permute-start | bytes 147464
  410.2 0.0 collective-permute-done
  410.2 6.0 %collective-permute-start.5 = (f32[16,768]{1,0:T(8,128)}, f32[16,768]{1,0:T(8,128)S(1)}, u32[]{:S(2)}, u32[]{:S(2)}) collective-permute-start(f32[16,768]{1,0:T(8,128)} %fusion), channel_id=1, source_target_pairs={{0,6},{1,7},{2,8},{3,9},{4,10},{5,11},{6,12},{7,13},{8,14},{9,15},... | collective-permute-start | bytes 147464
  416.2 0.0 collective-permute-done.1
  416.3 3.9 collective-permute-start.6
  420.2 1.3 dynamic-slice.4
  422.1 0.0 collective-permute-done.2
  422.1 0.0 collective-permute-done.3
  422.1 0.0 collective-permute-done.4
  422.1 0.0 collective-permute-done.5
  422.1 0.0 collective-permute-done.6
  422.2 1.8 concatenate
  424.0 0.0 copy-done.1
  424.0 1.4 fusion.12
Async XLA Ops:
  6.5 49.6 %copy-start = (bf16[768,1536]{1,0:T(8,128)(2,1)S(1)}, bf16[768,1536]{1,0:T(8,128)(2,1)}, u32[]{:S(2)}) copy-start(bf16[768,1536]{1,0:T(8,128)(2,1)} %param.6) | copy-start | bytes 7077892
  6.5 304.5 %all-reduce.4.cloned.1.call-start = ((), (), s32[]{:S(2)}) async-start(), calls=%async_computation | async-start | bytes 4718592 | tf_op jit(solution)/shard_map/psum | solution.py:10
  59.7 251.4 %copy-start.2 = (f32[1536]{0:T(1024)S(1)}, f32[1536]{0:T(1024)}, u32[]{:S(2)}) copy-start(f32[1536]{0:T(1024)} %param.7) | copy-start | bytes 18436
  59.7 364.3 %copy-start.1 = (f32[768]{0:T(1024)S(1)}, f32[768]{0:T(1024)}, u32[]{:S(2)}) copy-start(f32[768]{0:T(1024)} %param.9) | copy-start | bytes 9220
  397.6 12.6 %collective-permute-start = (f32[16,768]{1,0:T(8,128)}, f32[16,768]{1,0:T(8,128)S(1)}, u32[]{:S(2)}, u32[]{:S(2)}) collective-permute-start(f32[16,768]{1,0:T(8,128)} %fusion), channel_id=1, source_target_pairs={{0,1},{1,2},{2,3},{3,4},{4,5},{5,6},{6,7},{7,8},{8,9},{9,10},{10,1... | collective-permute-start | bytes 147464
  399.6 16.7 %collective-permute-start.1 = (f32[16,768]{1,0:T(8,128)}, f32[16,768]{1,0:T(8,128)S(1)}, u32[]{:S(2)}, u32[]{:S(2)}) collective-permute-start(f32[16,768]{1,0:T(8,128)} %fusion), channel_id=1, source_target_pairs={{0,2},{1,3},{2,4},{3,5},{4,6},{5,7},{6,8},{7,9},{8,10},{9,11},{10,... | collective-permute-start | bytes 147464
  401.7 3.9 collective-permute-start.7
  403.0 19.1 %collective-permute-start.2 = (f32[16,768]{1,0:T(8,128)}, f32[16,768]{1,0:T(8,128)S(1)}, u32[]{:S(2)}, u32[]{:S(2)}) collective-permute-start(f32[16,768]{1,0:T(8,128)} %fusion), channel_id=1, source_target_pairs={{0,3},{1,4},{2,5},{3,6},{4,7},{5,8},{6,9},{7,10},{8,11},{9,12},{10... | collective-permute-start | bytes 147464
  404.3 17.8 %collective-permute-start.3 = (f32[16,768]{1,0:T(8,128)}, f32[16,768]{1,0:T(8,128)S(1)}, u32[]{:S(2)}, u32[]{:S(2)}) collective-permute-start(f32[16,768]{1,0:T(8,128)} %fusion), channel_id=1, source_target_pairs={{0,4},{1,5},{2,6},{3,7},{4,8},{5,9},{6,10},{7,11},{8,12},{9,13},{1... | collective-permute-start | bytes 147464
  405.6 16.5 %collective-permute-start.4 = (f32[16,768]{1,0:T(8,128)}, f32[16,768]{1,0:T(8,128)S(1)}, u32[]{:S(2)}, u32[]{:S(2)}) collective-permute-start(f32[16,768]{1,0:T(8,128)} %fusion), channel_id=1, source_target_pairs={{0,5},{1,6},{2,7},{3,8},{4,9},{5,10},{6,11},{7,12},{8,13},{9,14},{... | collective-permute-start | bytes 147464
  410.2 11.9 %collective-permute-start.5 = (f32[16,768]{1,0:T(8,128)}, f32[16,768]{1,0:T(8,128)S(1)}, u32[]{:S(2)}, u32[]{:S(2)}) collective-permute-start(f32[16,768]{1,0:T(8,128)} %fusion), channel_id=1, source_target_pairs={{0,6},{1,7},{2,8},{3,9},{4,10},{5,11},{6,12},{7,13},{8,14},{9,15},... | collective-permute-start | bytes 147464
  416.3 5.9 %collective-permute-start.6 = (f32[16,768]{1,0:T(8,128)}, f32[16,768]{1,0:T(8,128)S(1)}, u32[]{:S(2)}, u32[]{:S(2)}) collective-permute-start(f32[16,768]{1,0:T(8,128)} %fusion), channel_id=1, source_target_pairs={{0,7},{1,8},{2,9},{3,10},{4,11},{5,12},{6,13},{7,14},{8,15},{9,16}... | collective-permute-start | bytes 147464
Sparse Core Ops, SparseCore 0:
  59.8 251.2 all-reduce.3
where the time goes:
time: 436 us; the launch traced here: 432 us
  waiting for transfers between devices  251 us (58%)
  blocking collectives  131 us (30%)
  starting transfers between devices  21.6 us (5%)
  between operations  14.2 us (3%)
  matrix products  7.51 us (2%)
  local copies, waits for them, and re-layouts  4.85 us (1%)
    psum x1, waiting for transfers between devices, on_device(): summed_up = lax.psum(partial_up, 'row')  251 us
    unnamed x1, blocking collectives  82.6 us
    all_gather x1, blocking collectives, on_device(): gathered = lax.all_gather(tokens, 'col', axis=0, tiled=True)  48.6 us
    unnamed x8, starting transfers between devices  21.6 us
  transfers between devices with their start and end apart: 9, of which 1 were waited for; matrix products, arithmetic and copies ran while one was open for 0% of the time, Pallas kernels for 0%

commit v1 on v0

v1 whole, which is shorter than its diff:
```python
import jax
import jax.numpy as jnp
from jax import lax
from jax.sharding import Mesh, PartitionSpec as P

AXES = {"z": 8, "h": 2, "x": 4, "y": 4, "c": 2}
ROW = ("z", "h")
COL = ("x", "y", "c")


def swap(value, axis):
    return lax.ppermute(value, axis, [(0, 1), (1, 0)])


def spread(value, axes, members):
    copies = jnp.broadcast_to(value, (members,) + value.shape)
    return lax.all_to_all(copies, axes, 0, 0)


def on_device(tokens, up_weight, up_bias, down_weight, down_bias):
    bf16, f32 = jnp.bfloat16, jnp.float32
    own, width = tokens.shape
    up_other = swap(up_weight, "c")
    bias_other = swap(up_bias, "c")
    down_other = swap(down_weight, "c")

    plane = spread(tokens, ("x", "y"), 16).reshape(16 * own, width)
    partial_up = jnp.concatenate(
        [
            jnp.dot(plane, up_weight, preferred_element_type=f32).astype(bf16),
            jnp.dot(plane, up_other, preferred_element_type=f32).astype(bf16),
        ],
        axis=1,
    )
    hidden = partial_up.shape[1]
    along_z = lax.all_to_all(partial_up.reshape(8, 2 * own, hidden), "z", 0, 0)
    summed_z = jnp.sum(along_z.astype(f32), axis=0)
    summed_up = summed_z + swap(summed_z.astype(bf16), "h").astype(f32)
    bias = jnp.concatenate([up_bias, bias_other])
    activated = jax.nn.gelu(summed_up + bias, approximate=True).astype(bf16)

    gathered = spread(activated, "z", 8).reshape(16 * own, hidden)
    half = hidden // 2
    partial_down = jnp.dot(gathered[:, :half], down_weight, preferred_element_type=f32) + jnp.dot(
        gathered[:, half:], down_other, preferred_element_type=f32
    )
    parts = lax.all_to_all(partial_down.astype(bf16).reshape(16, own, width), ("x", "y"), 0, 0)
    branch = jnp.sum(parts.astype(f32), axis=0)
    return (tokens.astype(f32) + branch + down_bias).astype(bf16)


def solution(mesh):
    fine = Mesh(mesh.devices.reshape(tuple(AXES.values())), tuple(AXES))
    placed = (P(COL, ROW), P(ROW, COL), P(COL), P(COL, ROW), P(ROW))
    return jax.shard_map(
        on_device, mesh=fine, in_specs=placed, out_specs=P(COL, ROW), check_vma=False
    )
```

time: 436 us -> 140 us (0.32)
  waiting for transfers between devices: 251 us -> 25.6 us
  blocking collectives: 131 us -> 72.3 us
  between operations: 14.2 us -> 0.15 us
  starting transfers between devices: 21.6 us -> 29.9 us
    psum x1 -> x0, waiting for transfers between devices: 251 us -> none  [on_device(): summed_up = lax.psum(partial_up, 'row')]
    unnamed x1 -> x0, blocking collectives: 82.6 us -> none
    all_to_all x0 -> x3, blocking collectives: none -> 72.3 us  [the longest x1 37.9 us: on_device(): along_z = lax.all_to_all(partial_up.reshape(8, 2 * own, hidden), 'z', 0, 0)]
    all_gather x1 -> x0, blocking collectives: 48.6 us -> none  [on_device(): gathered = lax.all_gather(tokens, 'col', axis=0, tiled=True)]
    all_to_all x0 -> x1, waiting for transfers between devices: none -> 24.8 us  [spread(): return lax.all_to_all(copies, axes, 0, 0)]
    ppermute x0 -> x4, starting transfers between devices: none -> 23.9 us  [swap(): return lax.ppermute(value, axis, [(0, 1), (1, 0)])]
    unnamed x8 -> x0, starting transfers between devices: 21.6 us -> none
    all_to_all x0 -> x1, starting transfers between devices: none -> 6 us  [spread(): return lax.all_to_all(copies, axes, 0, 0)]
  transfers between devices with their start and end apart: 9 -> 5, of which waited for: 1 -> 2; matrix products, arithmetic and copies ran while one was open for 0% -> 4% of each run, Pallas kernels for 0% -> 0%
where the time goes in v1:
time: 140 us; the launch traced here: 139 us
  blocking collectives  72.3 us (52%)
  starting transfers between devices  29.9 us (21%)
  waiting for transfers between devices  25.6 us (18%)
  matrix products  6.54 us (5%)
  local copies, waits for them, and re-layouts  3.02 us (2%)
  other arithmetic  1.87 us (1%)
    all_to_all x1, blocking collectives, on_device(): along_z = lax.all_to_all(partial_up.reshape(8, 2 * own, hidden), 'z', 0, 0)  37.9 us
    all_to_all x1, waiting for transfers between devices, spread(): return lax.all_to_all(copies, axes, 0, 0)  24.8 us
    ppermute x4, starting transfers between devices, swap(): return lax.ppermute(value, axis, [(0, 1), (1, 0)])  23.9 us
    all_to_all x1, blocking collectives, on_device(): lax.all_to_all(partial_down.astype(bf16).reshape(16, own, width), ('x', '...  18.2 us
    all_to_all x1, blocking collectives, spread(): return lax.all_to_all(copies, axes, 0, 0)  16.2 us
    all_to_all x1, starting transfers between devices, spread(): return lax.all_to_all(copies, axes, 0, 0)  6 us
  transfers between devices with their start and end apart: 5, of which 2 were waited for; matrix products, arithmetic and copies ran while one was open for 4% of the time, Pallas kernels for 0%

profile of v1, /device:TPU:1, one launch (start us, length us, event | category | flops | bytes accessed | tf_op | source)
XLA Modules:
  0.0 139.4 jit_solution(13651608978999933193)
XLA Ops:
  0.0 8.8 %collective-permute-start = (bf16[768,1536]{1,0:T(8,128)(2,1)}, bf16[768,1536]{1,0:T(8,128)(2,1)S(1)}, u32[]{:S(2)}, u32[]{:S(2)}) collective-permute-start(bf16[768,1536]{1,0:T(8,128)(2,1)} %param.6), channel_id=1, source_target_pairs={{0,1},{1,0},{2,3},{3,2},{4,5},{5,4},{6,7},{7,6},{8,9},{9,8},{10,11... | collective-permute-start | bytes 7077896 | tf_op jit(solution)/shard_map/ppermute | solution.py:12
  8.8 0.8 broadcast_in_dim.8
  9.6 16.2 %all_to_all.20 = bf16[16,12,768]{2,1,0:T(8,128)(2,1)S(1)} all-to-all(bf16[16,12,768]{2,1,0:T(8,128)(2,1)S(1)} %broadcast_in_dim.8), channel_id=1, replica_groups=mesh['z'=8,'h'=2,'x'=4,'y'=4,'c'=2] {'x','y'}, dimensions={0} | all-to-all | bytes 589824 | tf_op jit(solution)/shard_map/all_to_all | solution.py:17
  25.7 0.1 reshape.14
  25.8 2.3 %convolution_convert_fusion.1 = bf16[192,1536]{1,0:T(8,128)(2,1)S(1)} fusion(bf16[192,768]{1,0:T(8,128)(2,1)S(1)} %reshape.14, bf16[768,1536]{1,0:T(8,128)(2,1)} %param.6), kind=kOutput, calls=%fused_computation.1 | convolution fusion | flops 453279744 | bytes 3244032 | tf_op jit(solution)/shard_map/dot_general | solution.py:30
  28.1 0.0 collective-permute-done
  28.1 0.6 convolution_convert_fusion
  28.7 0.1 pad_maximum_fusion
  28.9 0.0 copy-start
  28.9 37.9 %all_to_all.21 = bf16[8,24,3072]{2,1,0:T(8,128)(2,1)S(1)} all-to-all(bf16[8,24,3072]{2,1,0:T(8,128)(2,1)S(1)} %bitcast.8), channel_id=1, replica_groups=mesh['z'=8,'h'=2,'x'=4,'y'=4,'c'=2] {'z'}, dimensions={0} | all-to-all | bytes 2359296 | tf_op jit(solution)/shard_map/all_to_all | solution.py:36
  66.8 0.2 convert_reduce_fusion
  67.0 4.7 %collective-permute-start.1 = (bf16[24,3072]{1,0:T(8,128)(2,1)S(1)}, bf16[24,3072]{1,0:T(8,128)(2,1)S(1)}, u32[]{:S(2)}, u32[]{:S(2)}) collective-permute-start(bf16[24,3072]{1,0:T(8,128)(2,1)S(1)} %convert_element_type.34), channel_id=1, source_target_pairs={{0,32},{32,0},{1,33},{33,1},{2,34},{34,2},{3,35},{35,3},{4,36},{36... | collective-permute-start | bytes 442376 | tf_op jit(solution)/shard_map/ppermute | solution.py:12
  71.7 0.0 copy-done
  71.7 5.3 %collective-permute-start.2 = (f32[1536]{0:T(1024)S(1)}, f32[1536]{0:T(1024)S(1)}, u32[]{:S(2)}, u32[]{:S(2)}) collective-permute-start(f32[1536]{0:T(1024)S(1)} %copy-done), channel_id=1, source_target_pairs={{0,1},{1,0},{2,3},{3,2},{4,5},{5,4},{6,7},{7,6},{8,9},{9,8},{10,11... | collective-permute-start | bytes 18440 | tf_op jit(solution)/shard_map/ppermute | solution.py:12
  77.0 0.8 collective-permute-done.2
  77.8 0.0 collective-permute-done.1
  77.9 0.1 fusion.11
  78.0 1.1 broadcast_in_dim.9
  79.1 6.0 %all-to-all-start.2 = ((bf16[8,24,3072]{2,1,0:T(8,128)(2,1)}), bf16[8,24,3072]{2,1,0:T(8,128)(2,1)S(1)}, u32[]{:S(2)}, u32[]{:S(2)}) async-start(bf16[8,24,3072]{2,1,0:T(8,128)(2,1)} %broadcast_in_dim.9), calls=%async_computation.2 | async-start | bytes 2359296 | tf_op jit(solution)/shard_map/all_to_all | solution.py:17
  85.1 5.1 %collective-permute-start.3 = (bf16[1536,768]{1,0:T(8,128)(2,1)}, bf16[1536,768]{1,0:T(8,128)(2,1)S(1)}, u32[]{:S(2)}, u32[]{:S(2)}) collective-permute-start(bf16[1536,768]{1,0:T(8,128)(2,1)} %param.8), channel_id=1, source_target_pairs={{0,1},{1,0},{2,3},{3,2},{4,5},{5,4},{6,7},{7,6},{8,9},{9,8},{10,11... | collective-permute-start | bytes 7077896 | tf_op jit(solution)/shard_map/ppermute | solution.py:12
  90.2 24.8 %all-to-all-done.2 = bf16[8,24,3072]{2,1,0:T(8,128)(2,1)S(1)} async-done(((bf16[8,24,3072]{2,1,0:T(8,128)(2,1)}), bf16[8,24,3072]{2,1,0:T(8,128)(2,1)S(1)}, u32[]{:S(2)}, u32[]{:S(2)}) %all-to-all-start.2) | async-done | bytes 1179680 | tf_op jit(solution)/shard_map/all_to_all | solution.py:17
  115.0 2.3 %fusion.2 = f32[192,768]{1,0:T(8,128)S(1)} fusion(bf16[1536,768]{1,0:T(8,128)(2,1)} %param.8, bf16[192,3072]{1,0:T(8,128)(2,1)S(1)} %bitcast.9), kind=kOutput, calls=%fused_computation.8 | convolution fusion | flops 452984832 | bytes 3538944 | tf_op jit(solution)/shard_map/dot_general | solution.py:44
  117.3 0.0 copy-start.1
  117.3 0.0 collective-permute-done.3
  117.4 1.3 fusion
  118.7 1.0 reshape.17
  119.7 18.2 %all_to_all.22 = bf16[16,12,768]{2,1,0:T(8,128)(2,1)S(1)} all-to-all(bf16[16,12,768]{2,1,0:T(8,128)(2,1)S(1)} %reshape.17), channel_id=1, replica_groups=mesh['z'=8,'h'=2,'x'=4,'y'=4,'c'=2] {'x','y'}, dimensions={0} | all-to-all | bytes 589824 | tf_op jit(solution)/shard_map/all_to_all | solution.py:47
  138.0 0.1 convert_reduce_fusion.1
  138.0 0.0 copy-done.1
  138.0 1.4 add_convert_fusion
  (2 shorter events, 0.0 us)
Async XLA Ops:
  0.0 28.1 %collective-permute-start = (bf16[768,1536]{1,0:T(8,128)(2,1)}, bf16[768,1536]{1,0:T(8,128)(2,1)S(1)}, u32[]{:S(2)}, u32[]{:S(2)}) collective-permute-start(bf16[768,1536]{1,0:T(8,128)(2,1)} %param.6), channel_id=1, source_target_pairs={{0,1},{1,0},{2,3},{3,2},{4,5},{5,4},{6,7},{7,6},{8,9},{9,8},{10,11... | collective-permute-start | bytes 7077896 | tf_op jit(solution)/shard_map/ppermute | solution.py:12
  28.9 42.9 %copy-start = (f32[1536]{0:T(1024)S(1)}, f32[1536]{0:T(1024)}, u32[]{:S(2)}) copy-start(f32[1536]{0:T(1024)} %param.7) | copy-start | bytes 18436
  67.0 10.9 %collective-permute-start.1 = (bf16[24,3072]{1,0:T(8,128)(2,1)S(1)}, bf16[24,3072]{1,0:T(8,128)(2,1)S(1)}, u32[]{:S(2)}, u32[]{:S(2)}) collective-permute-start(bf16[24,3072]{1,0:T(8,128)(2,1)S(1)} %convert_element_type.34), channel_id=1, source_target_pairs={{0,32},{32,0},{1,33},{33,1},{2,34},{34,2},{3,35},{35,3},{4,36},{36... | collective-permute-start | bytes 442376 | tf_op jit(solution)/shard_map/ppermute | solution.py:12
  71.7 6.1 %collective-permute-start.2 = (f32[1536]{0:T(1024)S(1)}, f32[1536]{0:T(1024)S(1)}, u32[]{:S(2)}, u32[]{:S(2)}) collective-permute-start(f32[1536]{0:T(1024)S(1)} %copy-done), channel_id=1, source_target_pairs={{0,1},{1,0},{2,3},{3,2},{4,5},{5,4},{6,7},{7,6},{8,9},{9,8},{10,11... | collective-permute-start | bytes 18440 | tf_op jit(solution)/shard_map/ppermute | solution.py:12
  79.1 35.9 %all-to-all-start.2 = ((bf16[8,24,3072]{2,1,0:T(8,128)(2,1)}), bf16[8,24,3072]{2,1,0:T(8,128)(2,1)S(1)}, u32[]{:S(2)}, u32[]{:S(2)}) async-start(bf16[8,24,3072]{2,1,0:T(8,128)(2,1)} %broadcast_in_dim.9), calls=%async_computation.2 | async-start | bytes 2359296 | tf_op jit(solution)/shard_map/all_to_all | solution.py:17
  85.1 32.2 %collective-permute-start.3 = (bf16[1536,768]{1,0:T(8,128)(2,1)}, bf16[1536,768]{1,0:T(8,128)(2,1)S(1)}, u32[]{:S(2)}, u32[]{:S(2)}) collective-permute-start(bf16[1536,768]{1,0:T(8,128)(2,1)} %param.8), channel_id=1, source_target_pairs={{0,1},{1,0},{2,3},{3,2},{4,5},{5,4},{6,7},{7,6},{8,9},{9,8},{10,11... | collective-permute-start | bytes 7077896 | tf_op jit(solution)/shard_map/ppermute | solution.py:12
  117.3 20.7 %copy-start.1 = (f32[768]{0:T(1024)S(1)}, f32[768]{0:T(1024)}, u32[]{:S(2)}) copy-start(f32[768]{0:T(1024)} %param.9) | copy-start | bytes 9220

commit v2 on v1

v2 whole, which is shorter than its diff:
```python
import jax
import jax.numpy as jnp
from jax import lax
from jax.sharding import Mesh, PartitionSpec as P

AXES = {"q": 4, "p": 2, "h": 2, "x": 4, "y": 4, "c": 2}
ROW = ("q", "p", "h")
COL = ("x", "y", "c")


def swap(value, axis):
    return lax.ppermute(value, axis, [(0, 1), (1, 0)])


def trade(value):
    def other(z, c):
        return (((z - c) % 8 ^ 1) + c) % 8

    pairs = [(z * 2 + c, other(z, c) * 2 + c) for z in range(8) for c in range(2)]
    return lax.ppermute(value, ("q", "p", "c"), pairs)


def tie(*values):
    tied = lax.optimization_barrier(values)
    return tied if len(values) > 1 else tied[0]


def spread(value, axes, members):
    copies = jnp.broadcast_to(value, (members,) + value.shape)
    return lax.all_to_all(copies, axes, 0, 0)


def on_device(tokens, up_weight, up_bias, down_weight, down_bias):
    bf16, f32 = jnp.bfloat16, jnp.float32
    own, width = tokens.shape
    even = lax.axis_index("p") == 0

    def keep_and_send(mine):
        other = swap(mine, "c")
        return jnp.where(even, mine, other), jnp.where(even, other, mine)

    gathered = spread(tokens, ("x", "y"), 16)
    up_keep, up_send = tie(*keep_and_send(up_weight))
    bias_keep, _ = keep_and_send(up_bias)
    down_keep, down_send = tie(*keep_and_send(down_weight))

    plane = gathered.reshape(16 * own, width)
    sent = jnp.dot(plane, up_send, preferred_element_type=f32).astype(bf16)
    kept = tie(jnp.dot(plane, up_keep, preferred_element_type=f32))
    pair_sum = (kept + trade(sent).astype(f32)).astype(bf16)
    parts_up = lax.all_to_all(pair_sum.reshape(4, 4 * own, -1), "q", 0, 0)
    summed_z = jnp.sum(parts_up.astype(f32), axis=0)
    halves = lax.all_gather(summed_z.astype(bf16), "h", axis=0)
    summed_up = summed_z + jnp.where(lax.axis_index("h") == 0, halves[1], halves[0]).astype(f32)
    activated = jax.nn.gelu(summed_up + bias_keep, approximate=True).astype(bf16)

    held = lax.all_gather(activated, "q", axis=0, tiled=True)
    partial_down = tie(jnp.dot(held, down_keep, preferred_element_type=f32)) + jnp.dot(
        trade(held), down_send, preferred_element_type=f32
    )
    parts = lax.all_to_all(partial_down.astype(bf16).reshape(16, own, width), ("x", "y"), 0, 0)
    branch = jnp.sum(parts.astype(f32), axis=0)
    return (tokens.astype(f32) + branch + down_bias).astype(bf16)


def solution(mesh):
    fine = Mesh(mesh.devices.reshape(tuple(AXES.values())), tuple(AXES))
    placed = (P(COL, ROW), P(ROW, COL), P(COL), P(COL, ROW), P(ROW))
    return jax.shard_map(
        on_device, mesh=fine, in_specs=placed, out_specs=P(COL, ROW), check_vma=False
    )
```

time: 140 us -> 124 us (0.89)
  blocking collectives: 72.3 us -> 38.4 us
  starting transfers between devices: 29.9 us -> 43.7 us
  waiting for transfers between devices: 25.6 us -> 31.1 us
  matrix products: 6.54 us -> 2.51 us
  other arithmetic: 1.87 us -> 5.84 us
    all_to_all x2 -> x0, blocking collectives: 54.1 us -> none  [the longest x1 37.9 us: on_device(): along_z = lax.all_to_all(partial_up.reshape(8, 2 * own, hidden), 'z', 0, 0)]
    ppermute x0 -> x2, starting transfers between devices: none -> 22 us  [trade(): return lax.ppermute(value, ('q', 'p', 'c'), pairs)]
    all_gather x0 -> x2, blocking collectives: none -> 21.8 us  [the longest x1 13.1 us: on_device(): held = lax.all_gather(activated, 'q', axis=0, tiled=True)]
    all_to_all x1, waiting for transfers between devices: 24.8 us -> 13.5 us  [spread(): return lax.all_to_all(copies, axes, 0, 0)]
    ppermute x4 -> x3, starting transfers between devices: 23.9 us -> 14.2 us  [swap(): return lax.ppermute(value, axis, [(0, 1), (1, 0)])]
    ppermute x0 -> x2, waiting for transfers between devices: none -> 9.29 us  [trade(): return lax.ppermute(value, ('q', 'p', 'c'), pairs)]
    all_to_all x0 -> x1, waiting for transfers between devices: none -> 7.5 us  [on_device(): parts_up = lax.all_to_all(pair_sum.reshape(4, 4 * own, -1), 'q', 0, 0)]
    dot_general x4, matrix products: 6.54 us -> 2.51 us  [the longest x1 0.63 us: on_device(): jnp.dot(trade(held), down_send, preferred_element_type=f32)]
  transfers between devices with their start and end apart: 5 -> 7, of which waited for: 2 -> 5; matrix products, arithmetic and copies ran while one was open for 4% -> 5% of each run, Pallas kernels for 0% -> 0%
where the time goes in v2:
time: 124 us; the launch traced here: 123 us
  starting transfers between devices  43.7 us (35%)
  blocking collectives  38.4 us (31%)
  waiting for transfers between devices  31.1 us (25%)
  other arithmetic  5.84 us (5%)
  matrix products  2.51 us (2%)
  local copies, waits for them, and re-layouts  1.66 us (1%)
    ppermute x2, starting transfers between devices, trade(): return lax.ppermute(value, ('q', 'p', 'c'), pairs)  22 us
    all_to_all x1, blocking collectives, on_device(): lax.all_to_all(partial_down.astype(bf16).reshape(16, own, width), ('x', '...  16.7 us
    ppermute x3, starting transfers between devices, swap(): return lax.ppermute(value, axis, [(0, 1), (1, 0)])  14.2 us
    all_to_all x1, waiting for transfers between devices, spread(): return lax.all_to_all(copies, axes, 0, 0)  13.5 us
    all_gather x1, blocking collectives, on_device(): held = lax.all_gather(activated, 'q', axis=0, tiled=True)  13.1 us
    ppermute x2, waiting for transfers between devices, trade(): return lax.ppermute(value, ('q', 'p', 'c'), pairs)  9.29 us
    all_gather x1, blocking collectives, on_device(): halves = lax.all_gather(summed_z.astype(bf16), 'h', axis=0)  8.68 us
    all_to_all x1, waiting for transfers between devices, on_device(): parts_up = lax.all_to_all(pair_sum.reshape(4, 4 * own, -1), 'q', 0, 0)  7.5 us
  transfers between devices with their start and end apart: 7, of which 5 were waited for; matrix products, arithmetic and copies ran while one was open for 5% of the time, Pallas kernels for 0%

profile of v2, /device:TPU:1, one launch (start us, length us, event | category | flops | bytes accessed | tf_op | source)
XLA Modules:
  0.0 123.5 jit_solution(4216444691270828403)
XLA Ops:
  0.0 8.8 %collective-permute-start = (bf16[768,1536]{1,0:T(8,128)(2,1)}, bf16[768,1536]{1,0:T(8,128)(2,1)S(1)}, u32[]{:S(2)}, u32[]{:S(2)}) collective-permute-start(bf16[768,1536]{1,0:T(8,128)(2,1)} %param.6), channel_id=1, source_target_pairs={{0,1},{1,0},{2,3},{3,2},{4,5},{5,4},{6,7},{7,6},{8,9},{9,8},{10,11... | collective-permute-start | bytes 7077896 | tf_op jit(solution)/shard_map/ppermute | solution.py:12
  8.8 1.5 %broadcast_in_dim.2 = bf16[16,12,768]{2,1,0:T(8,128)(2,1)} broadcast(bf16[12,768]{1,0:T(8,128)(2,1)} %param.5), dimensions={1,2} | broadcast | bytes 313344 | tf_op jit(solution)/shard_map/broadcast_in_dim | solution.py:29
  10.3 3.6 %all-to-all-start = ((bf16[16,12,768]{2,1,0:T(8,128)(2,1)}), bf16[16,12,768]{2,1,0:T(8,128)(2,1)S(1)}, u32[]{:S(2)}, u32[]{:S(2)}) async-start(bf16[16,12,768]{2,1,0:T(8,128)(2,1)} %broadcast_in_dim.2), calls=%async_computation | async-start | bytes 786432 | tf_op jit(solution)/shard_map/all_to_all | solution.py:30
  13.9 13.5 %all-to-all-done = bf16[16,12,768]{2,1,0:T(8,128)(2,1)S(1)} async-done(((bf16[16,12,768]{2,1,0:T(8,128)(2,1)}), bf16[16,12,768]{2,1,0:T(8,128)(2,1)S(1)}, u32[]{:S(2)}, u32[]{:S(2)}) %all-to-all-start) | async-done | bytes 294944 | tf_op jit(solution)/shard_map/all_to_all | solution.py:30
  27.4 0.1 reshape.23
  27.4 0.0 collective-permute-done
  27.4 2.0 %broadcast_select_fusion.2 = (bf16[768,1536]{1,0:T(8,128)(2,1)S(1)}, bf16[768,1536]{1,0:T(8,128)(2,1)S(1)}) fusion(bf16[768,1536]{1,0:T(8,128)(2,1)S(1)} %collective-permute-done, bf16[768,1536]{1,0:T(8,128)(2,1)} %param.6, pred[]{:T(512)S(6)} %eq.6), kind=kLoop, calls=%fused_computation.5 | loop fusion | flops 2359296 | bytes 9437185 | tf_op jit(solution)/shard_map/jit(_where)/select_n | solution.py:40
  29.4 0.0 copy-start
  29.4 0.6 fusion
  30.1 8.8 %collective-permute-start.1 = (bf16[192,1536]{1,0:T(8,128)(2,1)S(1)}, bf16[192,1536]{1,0:T(8,128)(2,1)S(1)}, u32[]{:S(2)}, u32[]{:S(2)}) collective-permute-start(bf16[192,1536]{1,0:T(8,128)(2,1)S(1)} %fusion), channel_id=1, source_target_pairs={{0,64},{1,449},{64,0},{65,129},{128,192},{129,65},{192,128},{193,2... | collective-permute-start | bytes 1769480 | tf_op jit(solution)/shard_map/ppermute | solution.py:20
  38.8 0.0 copy-done
  38.8 1.9 %collective-permute-start.3 = (bf16[1536,768]{1,0:T(8,128)(2,1)S(1)}, bf16[1536,768]{1,0:T(8,128)(2,1)}, u32[]{:S(2)}, u32[]{:S(2)}) collective-permute-start(bf16[1536,768]{1,0:T(8,128)(2,1)S(1)} %copy-done), channel_id=1, source_target_pairs={{0,1},{1,0},{2,3},{3,2},{4,5},{5,4},{6,7},{7,6},{8,9},{9,8},{10,11... | collective-permute-start | bytes 7077896 | tf_op jit(solution)/shard_map/ppermute | solution.py:12
  40.8 0.6 convolution_bitcast_fusion
  41.4 0.0 copy-start.2
  41.4 4.7 %collective-permute-done.1 = bf16[192,1536]{1,0:T(8,128)(2,1)S(1)} collective-permute-done((bf16[192,1536]{1,0:T(8,128)(2,1)S(1)}, bf16[192,1536]{1,0:T(8,128)(2,1)S(1)}, u32[]{:S(2)}, u32[]{:S(2)}) %collective-permute-start.1) | collective-permute-done | bytes 589856 | tf_op jit(solution)/shard_map/ppermute | solution.py:20
  46.1 0.9 add_convert_fusion
  47.0 3.9 %all-to-all-start.1 = ((bf16[4,48,1536]{2,1,0:T(8,128)(2,1)}), bf16[4,48,1536]{2,1,0:T(8,128)(2,1)S(1)}, u32[]{:S(2)}, u32[]{:S(2)}) async-start(bf16[4,48,1536]{2,1,0:T(8,128)(2,1)} %bitcast.2), calls=%async_computation.1 | async-start | bytes 1179648 | tf_op jit(solution)/shard_map/all_to_all | solution.py:51
  50.9 0.0 copy-done.2
  50.9 3.5 %collective-permute-start.2 = (f32[1536]{0:T(1024)S(1)}, f32[1536]{0:T(1024)S(1)}, u32[]{:S(2)}, u32[]{:S(2)}) collective-permute-start(f32[1536]{0:T(1024)S(1)} %copy-done.2), channel_id=1, source_target_pairs={{0,1},{1,0},{2,3},{3,2},{4,5},{5,4},{6,7},{7,6},{8,9},{9,8},{10,11... | collective-permute-start | bytes 18440 | tf_op jit(solution)/shard_map/ppermute | solution.py:12
  54.5 0.8 collective-permute-done.2
  55.3 7.5 %all-to-all-done.1 = bf16[4,48,1536]{2,1,0:T(8,128)(2,1)S(1)} async-done(((bf16[4,48,1536]{2,1,0:T(8,128)(2,1)}), bf16[4,48,1536]{2,1,0:T(8,128)(2,1)S(1)}, u32[]{:S(2)}, u32[]{:S(2)}) %all-to-all-start.1) | async-done | bytes 589856 | tf_op jit(solution)/shard_map/all_to_all | solution.py:51
  62.8 0.1 convert_reduce_fusion
  62.9 8.7 %all-gather = bf16[96,1536]{1,0:T(8,128)(2,1)S(1)} all-gather(bf16[48,1536]{1,0:T(8,128)(2,1)S(1)} %convert_element_type.55), channel_id=2, replica_groups=mesh['q'=4,'p'=2,'h'=2,'x'=4,'y'=4,'c'=2] {'h'}, dimensions={0}, use_global_device_ids=true | all-gather | bytes 442368 | tf_op jit(solution)/shard_map/all_gather | solution.py:53
  71.6 0.1 fusion.9
  71.7 13.1 %all_gather.8 = bf16[192,1536]{1,0:T(8,128)(2,1)S(1)} all-gather(bf16[48,1536]{1,0:T(8,128)(2,1)S(1)} %fusion.9), channel_id=1, replica_groups=mesh['q'=4,'p'=2,'h'=2,'x'=4,'y'=4,'c'=2] {'q'}, dimensions={0}, use_global_device_ids=true | all-gather | bytes 737280 | tf_op jit(solution)/shard_map/all_gather | solution.py:57
  84.8 13.3 %collective-permute-start.4 = (bf16[192,1536]{1,0:T(8,128)(2,1)S(1)}, bf16[192,1536]{1,0:T(8,128)(2,1)S(1)}, u32[]{:S(2)}, u32[]{:S(2)}) collective-permute-start(bf16[192,1536]{1,0:T(8,128)(2,1)S(1)} %all_gather.8), channel_id=1, source_target_pairs={{0,64},{1,449},{64,0},{65,129},{128,192},{129,65},{192,128},{193,2... | collective-permute-start | bytes 1769480 | tf_op jit(solution)/shard_map/ppermute | solution.py:20
  98.1 0.0 collective-permute-done.3
  98.1 2.0 %broadcast_select_fusion = (bf16[1536,768]{1,0:T(8,128)(2,1)S(1)}, bf16[1536,768]{1,0:T(8,128)(2,1)S(1)}) fusion(bf16[1536,768]{1,0:T(8,128)(2,1)} %collective-permute-done.3, bf16[1536,768]{1,0:T(8,128)(2,1)S(1)} %copy-done, pred[]{:T(512)S(6)} %eq.6), kind=kLoop, calls=%fused_computation.3 | loop fusion | flops 2359296 | bytes 9437185 | tf_op jit(solution)/shard_map/jit(_where)/select_n | solution.py:40
  100.1 0.6 fusion.11
  100.7 0.0 copy-start.1
  100.8 0.0 copy-start.3
  100.8 4.6 %collective-permute-done.4 = bf16[192,1536]{1,0:T(8,128)(2,1)S(1)} collective-permute-done((bf16[192,1536]{1,0:T(8,128)(2,1)S(1)}, bf16[192,1536]{1,0:T(8,128)(2,1)S(1)}, u32[]{:S(2)}, u32[]{:S(2)}) %collective-permute-start.4) | collective-permute-done | bytes 589856 | tf_op jit(solution)/shard_map/ppermute | solution.py:20
  105.4 0.6 fusion.1
  106.0 0.1 reshape.25
  106.1 16.7 %all_to_all.15 = bf16[16,12,768]{2,1,0:T(8,128)(2,1)S(1)} all-to-all(bf16[16,12,768]{2,1,0:T(8,128)(2,1)S(1)} %reshape.25), channel_id=1, replica_groups=mesh['q'=4,'p'=2,'h'=2,'x'=4,'y'=4,'c'=2] {'x','y'}, dimensions={0} | all-to-all | bytes 589824 | tf_op jit(solution)/shard_map/all_to_all | solution.py:61
  122.8 0.1 convert_reduce_fusion.1
  122.8 0.0 copy-done.1
  122.8 0.0 copy-done.3
  122.8 0.6 add_convert_fusion.1
  (2 shorter events, 0.0 us)
Async XLA Ops:
  0.0 27.4 %collective-permute-start = (bf16[768,1536]{1,0:T(8,128)(2,1)}, bf16[768,1536]{1,0:T(8,128)(2,1)S(1)}, u32[]{:S(2)}, u32[]{:S(2)}) collective-permute-start(bf16[768,1536]{1,0:T(8,128)(2,1)} %param.6), channel_id=1, source_target_pairs={{0,1},{1,0},{2,3},{3,2},{4,5},{5,4},{6,7},{7,6},{8,9},{9,8},{10,11... | collective-permute-start | bytes 7077896 | tf_op jit(solution)/shard_map/ppermute | solution.py:12
  10.3 17.1 %all-to-all-start = ((bf16[16,12,768]{2,1,0:T(8,128)(2,1)}), bf16[16,12,768]{2,1,0:T(8,128)(2,1)S(1)}, u32[]{:S(2)}, u32[]{:S(2)}) async-start(bf16[16,12,768]{2,1,0:T(8,128)(2,1)} %broadcast_in_dim.2), calls=%async_computation | async-start | bytes 786432 | tf_op jit(solution)/shard_map/all_to_all | solution.py:30
  29.4 9.4 %copy-start = (bf16[1536,768]{1,0:T(8,128)(2,1)S(1)}, bf16[1536,768]{1,0:T(8,128)(2,1)}, u32[]{:S(2)}) copy-start(bf16[1536,768]{1,0:T(8,128)(2,1)} %param.8) | copy-start | bytes 7077892
  30.1 16.0 %collective-permute-start.1 = (bf16[192,1536]{1,0:T(8,128)(2,1)S(1)}, bf16[192,1536]{1,0:T(8,128)(2,1)S(1)}, u32[]{:S(2)}, u32[]{:S(2)}) collective-permute-start(bf16[192,1536]{1,0:T(8,128)(2,1)S(1)} %fusion), channel_id=1, source_target_pairs={{0,64},{1,449},{64,0},{65,129},{128,192},{129,65},{192,128},{193,2... | collective-permute-start | bytes 1769480 | tf_op jit(solution)/shard_map/ppermute | solution.py:20
  38.8 59.3 %collective-permute-start.3 = (bf16[1536,768]{1,0:T(8,128)(2,1)S(1)}, bf16[1536,768]{1,0:T(8,128)(2,1)}, u32[]{:S(2)}, u32[]{:S(2)}) collective-permute-start(bf16[1536,768]{1,0:T(8,128)(2,1)S(1)} %copy-done), channel_id=1, source_target_pairs={{0,1},{1,0},{2,3},{3,2},{4,5},{5,4},{6,7},{7,6},{8,9},{9,8},{10,11... | collective-permute-start | bytes 7077896 | tf_op jit(solution)/shard_map/ppermute | solution.py:12
  41.4 9.5 %copy-start.2 = (f32[1536]{0:T(1024)S(1)}, f32[1536]{0:T(1024)}, u32[]{:S(2)}) copy-start(f32[1536]{0:T(1024)} %param.7) | copy-start | bytes 18436
  47.0 15.8 %all-to-all-start.1 = ((bf16[4,48,1536]{2,1,0:T(8,128)(2,1)}), bf16[4,48,1536]{2,1,0:T(8,128)(2,1)S(1)}, u32[]{:S(2)}, u32[]{:S(2)}) async-start(bf16[4,48,1536]{2,1,0:T(8,128)(2,1)} %bitcast.2), calls=%async_computation.1 | async-start | bytes 1179648 | tf_op jit(solution)/shard_map/all_to_all | solution.py:51
  50.9 4.4 %collective-permute-start.2 = (f32[1536]{0:T(1024)S(1)}, f32[1536]{0:T(1024)S(1)}, u32[]{:S(2)}, u32[]{:S(2)}) collective-permute-start(f32[1536]{0:T(1024)S(1)} %copy-done.2), channel_id=1, source_target_pairs={{0,1},{1,0},{2,3},{3,2},{4,5},{5,4},{6,7},{7,6},{8,9},{9,8},{10,11... | collective-permute-start | bytes 18440 | tf_op jit(solution)/shard_map/ppermute | solution.py:12
  84.8 20.5 %collective-permute-start.4 = (bf16[192,1536]{1,0:T(8,128)(2,1)S(1)}, bf16[192,1536]{1,0:T(8,128)(2,1)S(1)}, u32[]{:S(2)}, u32[]{:S(2)}) collective-permute-start(bf16[192,1536]{1,0:T(8,128)(2,1)S(1)} %all_gather.8), channel_id=1, source_target_pairs={{0,64},{1,449},{64,0},{65,129},{128,192},{129,65},{192,128},{193,2... | collective-permute-start | bytes 1769480 | tf_op jit(solution)/shard_map/ppermute | solution.py:20
  100.7 22.1 %copy-start.1 = (bf16[12,768]{1,0:T(8,128)(2,1)S(1)}, bf16[12,768]{1,0:T(8,128)(2,1)}, u32[]{:S(2)}) copy-start(bf16[12,768]{1,0:T(8,128)(2,1)} %param.5) | copy-start | bytes 55300
  100.8 22.1 %copy-start.3 = (f32[768]{0:T(1024)S(1)}, f32[768]{0:T(1024)}, u32[]{:S(2)}) copy-start(f32[768]{0:T(1024)} %param.9) | copy-start | bytes 9220

commit v3 on v2

--- a/solution.py
+++ b/solution.py
@@ -20,14 +20,17 @@
     return lax.ppermute(value, ("q", "p", "c"), pairs)
 
 
+FIRST = 10
+PLANE = [[(k + FIRST) % 16 * 2 + c for k in range(16)] for c in range(2)]
+
+
+def in_plane(members):
+    return lax.all_to_all(members, COL, 0, 0, axis_index_groups=PLANE)
+
+
 def tie(*values):
     tied = lax.optimization_barrier(values)
     return tied if len(values) > 1 else tied[0]
-
-
-def spread(value, axes, members):
-    copies = jnp.broadcast_to(value, (members,) + value.shape)
-    return lax.all_to_all(copies, axes, 0, 0)
 
 
 def on_device(tokens, up_weight, up_bias, down_weight, down_bias):
@@ -39,7 +42,7 @@
         other = swap(mine, "c")
         return jnp.where(even, mine, other), jnp.where(even, other, mine)
 
-    gathered = spread(tokens, ("x", "y"), 16)
+    gathered = in_plane(jnp.broadcast_to(tokens, (16, own, width)))
     up_keep, up_send = tie(*keep_and_send(up_weight))
     bias_keep, _ = keep_and_send(up_bias)
     down_keep, down_send = tie(*keep_and_send(down_weight))
@@ -58,7 +61,7 @@
     partial_down = tie(jnp.dot(held, down_keep, preferred_element_type=f32)) + jnp.dot(
         trade(held), down_send, preferred_element_type=f32
     )
-    parts = lax.all_to_all(partial_down.astype(bf16).reshape(16, own, width), ("x", "y"), 0, 0)
+    parts = in_plane(partial_down.astype(bf16).reshape(16, own, width))
     branch = jnp.sum(parts.astype(f32), axis=0)
     return (tokens.astype(f32) + branch + down_bias).astype(bf16)
 

time: 124 us -> 121 us (0.976)
  the two profiles are of different devices: /device:TPU:1 before, /device:TPU:56 now
where the time goes in v3:
time: 121 us; the launch traced here: 120 us
  blocking collectives  42.4 us (35%)
  starting transfers between devices  38.2 us (32%)
  waiting for transfers between devices  29.3 us (24%)
  other arithmetic  5.84 us (5%)
  matrix products  2.51 us (2%)
  local copies, waits for them, and re-layouts  1.66 us (1%)
    all_gather x1, blocking collectives, on_device(): held = lax.all_gather(activated, 'q', axis=0, tiled=True)  16.6 us
    all_to_all x1, blocking collectives, in_plane(): return lax.all_to_all(members, COL, 0, 0, axis_index_groups=PLANE)  15.5 us
    all_to_all x1, waiting for transfers between devices, on_device(): parts_up = lax.all_to_all(pair_sum.reshape(4, 4 * own, -1), 'q', 0, 0)  12.1 us
    ppermute x3, starting transfers between devices, swap(): return lax.ppermute(value, axis, [(0, 1), (1, 0)])  11.2 us
    all_to_all x1, waiting for transfers between devices, in_plane(): return lax.all_to_all(members, COL, 0, 0, axis_index_groups=PLANE)  10.9 us
    all_gather x1, blocking collectives, on_device(): halves = lax.all_gather(summed_z.astype(bf16), 'h', axis=0)  10.3 us
    all_to_all x1, starting transfers between devices, on_device(): parts_up = lax.all_to_all(pair_sum.reshape(4, 4 * own, -1), 'q', 0, 0)  9.72 us
    ppermute x2, starting transfers between devices, trade(): return lax.ppermute(value, ('q', 'p', 'c'), pairs)  9.41 us
  transfers between devices with their start and end apart: 7, of which 4 were waited for; matrix products, arithmetic and copies ran while one was open for 5% of the time, Pallas kernels for 0%

profile of v3, /device:TPU:56, one launch (start us, length us, event | category | flops | bytes accessed | tf_op | source)
XLA Modules:
  0.0 120.2 jit_solution(16458613042843825649)
XLA Ops:
  0.0 1.9 %collective-permute-start = (bf16[768,1536]{1,0:T(8,128)(2,1)}, bf16[768,1536]{1,0:T(8,128)(2,1)S(1)}, u32[]{:S(2)}, u32[]{:S(2)}) collective-permute-start(bf16[768,1536]{1,0:T(8,128)(2,1)} %param.6), channel_id=1, source_target_pairs={{0,1},{1,0},{2,3},{3,2},{4,5},{5,4},{6,7},{7,6},{8,9},{9,8},{10,11... | collective-permute-start | bytes 7077896 | tf_op jit(solution)/shard_map/ppermute | solution.py:12
  1.9 1.5 %broadcast_in_dim.2 = bf16[16,12,768]{2,1,0:T(8,128)(2,1)} broadcast(bf16[12,768]{1,0:T(8,128)(2,1)} %param.5), dimensions={1,2} | broadcast | bytes 313344 | tf_op jit(solution)/shard_map/broadcast_in_dim | solution.py:45
  3.4 7.9 %all-to-all-start = ((bf16[16,12,768]{2,1,0:T(8,128)(2,1)}), bf16[16,12,768]{2,1,0:T(8,128)(2,1)S(1)}, u32[]{:S(2)}, u32[]{:S(2)}) async-start(bf16[16,12,768]{2,1,0:T(8,128)(2,1)} %broadcast_in_dim.2), calls=%async_computation | async-start | bytes 786432 | tf_op jit(solution)/shard_map/all_to_all | solution.py:28
  11.3 10.9 %all-to-all-done = bf16[16,12,768]{2,1,0:T(8,128)(2,1)S(1)} async-done(((bf16[16,12,768]{2,1,0:T(8,128)(2,1)}), bf16[16,12,768]{2,1,0:T(8,128)(2,1)S(1)}, u32[]{:S(2)}, u32[]{:S(2)}) %all-to-all-start) | async-done | bytes 294944 | tf_op jit(solution)/shard_map/all_to_all | solution.py:28
  22.2 0.1 reshape.23
  22.2 0.0 collective-permute-done
  22.2 2.0 %broadcast_select_fusion.2 = (bf16[768,1536]{1,0:T(8,128)(2,1)S(1)}, bf16[768,1536]{1,0:T(8,128)(2,1)S(1)}) fusion(bf16[768,1536]{1,0:T(8,128)(2,1)S(1)} %collective-permute-done, bf16[768,1536]{1,0:T(8,128)(2,1)} %param.6, pred[]{:T(512)S(6)} %eq.6), kind=kLoop, calls=%fused_computation.5 | loop fusion | flops 2359296 | bytes 9437185 | tf_op jit(solution)/shard_map/jit(_where)/select_n | solution.py:43
  24.2 0.0 copy-start
  24.2 0.6 fusion
  24.9 4.4 %collective-permute-start.1 = (bf16[192,1536]{1,0:T(8,128)(2,1)S(1)}, bf16[192,1536]{1,0:T(8,128)(2,1)S(1)}, u32[]{:S(2)}, u32[]{:S(2)}) collective-permute-start(bf16[192,1536]{1,0:T(8,128)(2,1)S(1)} %fusion), channel_id=1, source_target_pairs={{0,64},{1,449},{64,0},{65,129},{128,192},{129,65},{192,128},{193,2... | collective-permute-start | bytes 1769480 | tf_op jit(solution)/shard_map/ppermute | solution.py:20
  29.3 0.0 copy-done
  29.3 7.4 %collective-permute-start.3 = (bf16[1536,768]{1,0:T(8,128)(2,1)S(1)}, bf16[1536,768]{1,0:T(8,128)(2,1)}, u32[]{:S(2)}, u32[]{:S(2)}) collective-permute-start(bf16[1536,768]{1,0:T(8,128)(2,1)S(1)} %copy-done), channel_id=1, source_target_pairs={{0,1},{1,0},{2,3},{3,2},{4,5},{5,4},{6,7},{7,6},{8,9},{9,8},{10,11... | collective-permute-start | bytes 7077896 | tf_op jit(solution)/shard_map/ppermute | solution.py:12
  36.7 0.6 convolution_bitcast_fusion
  37.3 0.0 copy-start.2
  37.4 0.0 collective-permute-done.1
  37.4 0.9 add_convert_fusion
  38.3 9.7 %all-to-all-start.1 = ((bf16[4,48,1536]{2,1,0:T(8,128)(2,1)}), bf16[4,48,1536]{2,1,0:T(8,128)(2,1)S(1)}, u32[]{:S(2)}, u32[]{:S(2)}) async-start(bf16[4,48,1536]{2,1,0:T(8,128)(2,1)} %bitcast.2), calls=%async_computation.1 | async-start | bytes 1179648 | tf_op jit(solution)/shard_map/all_to_all | solution.py:54
  48.0 0.0 copy-done.2
  48.0 1.9 %collective-permute-start.2 = (f32[1536]{0:T(1024)S(1)}, f32[1536]{0:T(1024)S(1)}, u32[]{:S(2)}, u32[]{:S(2)}) collective-permute-start(f32[1536]{0:T(1024)S(1)} %copy-done.2), channel_id=1, source_target_pairs={{0,1},{1,0},{2,3},{3,2},{4,5},{5,4},{6,7},{7,6},{8,9},{9,8},{10,11... | collective-permute-start | bytes 18440 | tf_op jit(solution)/shard_map/ppermute | solution.py:12
  49.9 1.1 collective-permute-done.2
  51.1 12.1 %all-to-all-done.1 = bf16[4,48,1536]{2,1,0:T(8,128)(2,1)S(1)} async-done(((bf16[4,48,1536]{2,1,0:T(8,128)(2,1)}), bf16[4,48,1536]{2,1,0:T(8,128)(2,1)S(1)}, u32[]{:S(2)}, u32[]{:S(2)}) %all-to-all-start.1) | async-done | bytes 589856 | tf_op jit(solution)/shard_map/all_to_all | solution.py:54
  63.2 0.1 convert_reduce_fusion
  63.3 10.3 %all-gather = bf16[96,1536]{1,0:T(8,128)(2,1)S(1)} all-gather(bf16[48,1536]{1,0:T(8,128)(2,1)S(1)} %convert_element_type.55), channel_id=2, replica_groups=mesh['q'=4,'p'=2,'h'=2,'x'=4,'y'=4,'c'=2] {'h'}, dimensions={0}, use_global_device_ids=true | all-gather | bytes 442368 | tf_op jit(solution)/shard_map/all_gather | solution.py:56
  73.7 0.1 fusion.9
  73.8 16.6 %all_gather.8 = bf16[192,1536]{1,0:T(8,128)(2,1)S(1)} all-gather(bf16[48,1536]{1,0:T(8,128)(2,1)S(1)} %fusion.9), channel_id=1, replica_groups=mesh['q'=4,'p'=2,'h'=2,'x'=4,'y'=4,'c'=2] {'q'}, dimensions={0}, use_global_device_ids=true | all-gather | bytes 737280 | tf_op jit(solution)/shard_map/all_gather | solution.py:60
  90.4 5.0 %collective-permute-start.4 = (bf16[192,1536]{1,0:T(8,128)(2,1)S(1)}, bf16[192,1536]{1,0:T(8,128)(2,1)S(1)}, u32[]{:S(2)}, u32[]{:S(2)}) collective-permute-start(bf16[192,1536]{1,0:T(8,128)(2,1)S(1)} %all_gather.8), channel_id=1, source_target_pairs={{0,64},{1,449},{64,0},{65,129},{128,192},{129,65},{192,128},{193,2... | collective-permute-start | bytes 1769480 | tf_op jit(solution)/shard_map/ppermute | solution.py:20
  95.4 0.0 collective-permute-done.3
  95.4 2.0 %broadcast_select_fusion = (bf16[1536,768]{1,0:T(8,128)(2,1)S(1)}, bf16[1536,768]{1,0:T(8,128)(2,1)S(1)}) fusion(bf16[1536,768]{1,0:T(8,128)(2,1)} %collective-permute-done.3, bf16[1536,768]{1,0:T(8,128)(2,1)S(1)} %copy-done, pred[]{:T(512)S(6)} %eq.6), kind=kLoop, calls=%fused_computation.3 | loop fusion | flops 2359296 | bytes 9437185 | tf_op jit(solution)/shard_map/jit(_where)/select_n | solution.py:43
  97.4 0.6 fusion.11
  98.0 0.0 copy-start.1
  98.0 0.0 copy-start.3
  98.1 5.2 %collective-permute-done.4 = bf16[192,1536]{1,0:T(8,128)(2,1)S(1)} collective-permute-done((bf16[192,1536]{1,0:T(8,128)(2,1)S(1)}, bf16[192,1536]{1,0:T(8,128)(2,1)S(1)}, u32[]{:S(2)}, u32[]{:S(2)}) %collective-permute-start.4) | collective-permute-done | bytes 589856 | tf_op jit(solution)/shard_map/ppermute | solution.py:20
  103.3 0.6 fusion.1
  103.9 0.1 reshape.25
  104.0 15.5 %all_to_all.15 = bf16[16,12,768]{2,1,0:T(8,128)(2,1)S(1)} all-to-all(bf16[16,12,768]{2,1,0:T(8,128)(2,1)S(1)} %reshape.25), channel_id=1, replica_groups={{20,22,24,26,28,30,0,2,4,6,8,10,12,14,16,18},{21,23,25,27,29,31,1,3,5,7..., dimensions={0} | all-to-all | bytes 589824 | tf_op jit(solution)/shard_map/all_to_all | solution.py:28
  119.4 0.1 convert_reduce_fusion.1
  119.5 0.0 copy-done.1
  119.5 0.0 copy-done.3
  119.5 0.6 add_convert_fusion.1
  (2 shorter events, 0.0 us)
Async XLA Ops:
  0.0 22.2 %collective-permute-start = (bf16[768,1536]{1,0:T(8,128)(2,1)}, bf16[768,1536]{1,0:T(8,128)(2,1)S(1)}, u32[]{:S(2)}, u32[]{:S(2)}) collective-permute-start(bf16[768,1536]{1,0:T(8,128)(2,1)} %param.6), channel_id=1, source_target_pairs={{0,1},{1,0},{2,3},{3,2},{4,5},{5,4},{6,7},{7,6},{8,9},{9,8},{10,11... | collective-permute-start | bytes 7077896 | tf_op jit(solution)/shard_map/ppermute | solution.py:12
  3.4 18.7 %all-to-all-start = ((bf16[16,12,768]{2,1,0:T(8,128)(2,1)}), bf16[16,12,768]{2,1,0:T(8,128)(2,1)S(1)}, u32[]{:S(2)}, u32[]{:S(2)}) async-start(bf16[16,12,768]{2,1,0:T(8,128)(2,1)} %broadcast_in_dim.2), calls=%async_computation | async-start | bytes 786432 | tf_op jit(solution)/shard_map/all_to_all | solution.py:28
  24.2 5.1 %copy-start = (bf16[1536,768]{1,0:T(8,128)(2,1)S(1)}, bf16[1536,768]{1,0:T(8,128)(2,1)}, u32[]{:S(2)}) copy-start(bf16[1536,768]{1,0:T(8,128)(2,1)} %param.8) | copy-start | bytes 7077892
  24.9 12.5 %collective-permute-start.1 = (bf16[192,1536]{1,0:T(8,128)(2,1)S(1)}, bf16[192,1536]{1,0:T(8,128)(2,1)S(1)}, u32[]{:S(2)}, u32[]{:S(2)}) collective-permute-start(bf16[192,1536]{1,0:T(8,128)(2,1)S(1)} %fusion), channel_id=1, source_target_pairs={{0,64},{1,449},{64,0},{65,129},{128,192},{129,65},{192,128},{193,2... | collective-permute-start | bytes 1769480 | tf_op jit(solution)/shard_map/ppermute | solution.py:20
  29.3 66.1 %collective-permute-start.3 = (bf16[1536,768]{1,0:T(8,128)(2,1)S(1)}, bf16[1536,768]{1,0:T(8,128)(2,1)}, u32[]{:S(2)}, u32[]{:S(2)}) collective-permute-start(bf16[1536,768]{1,0:T(8,128)(2,1)S(1)} %copy-done), channel_id=1, source_target_pairs={{0,1},{1,0},{2,3},{3,2},{4,5},{5,4},{6,7},{7,6},{8,9},{9,8},{10,11... | collective-permute-start | bytes 7077896 | tf_op jit(solution)/shard_map/ppermute | solution.py:12
  37.3 10.7 %copy-start.2 = (f32[1536]{0:T(1024)S(1)}, f32[1536]{0:T(1024)}, u32[]{:S(2)}) copy-start(f32[1536]{0:T(1024)} %param.7) | copy-start | bytes 18436
  38.3 24.9 %all-to-all-start.1 = ((bf16[4,48,1536]{2,1,0:T(8,128)(2,1)}), bf16[4,48,1536]{2,1,0:T(8,128)(2,1)S(1)}, u32[]{:S(2)}, u32[]{:S(2)}) async-start(bf16[4,48,1536]{2,1,0:T(8,128)(2,1)} %bitcast.2), calls=%async_computation.1 | async-start | bytes 1179648 | tf_op jit(solution)/shard_map/all_to_all | solution.py:54
  48.0 3.1 %collective-permute-start.2 = (f32[1536]{0:T(1024)S(1)}, f32[1536]{0:T(1024)S(1)}, u32[]{:S(2)}, u32[]{:S(2)}) collective-permute-start(f32[1536]{0:T(1024)S(1)} %copy-done.2), channel_id=1, source_target_pairs={{0,1},{1,0},{2,3},{3,2},{4,5},{5,4},{6,7},{7,6},{8,9},{9,8},{10,11... | collective-permute-start | bytes 18440 | tf_op jit(solution)/shard_map/ppermute | solution.py:12
  90.4 12.9 %collective-permute-start.4 = (bf16[192,1536]{1,0:T(8,128)(2,1)S(1)}, bf16[192,1536]{1,0:T(8,128)(2,1)S(1)}, u32[]{:S(2)}, u32[]{:S(2)}) collective-permute-start(bf16[192,1536]{1,0:T(8,128)(2,1)S(1)} %all_gather.8), channel_id=1, source_target_pairs={{0,64},{1,449},{64,0},{65,129},{128,192},{129,65},{192,128},{193,2... | collective-permute-start | bytes 1769480 | tf_op jit(solution)/shard_map/ppermute | solution.py:20
  98.0 21.5 %copy-start.1 = (bf16[12,768]{1,0:T(8,128)(2,1)S(1)}, bf16[12,768]{1,0:T(8,128)(2,1)}, u32[]{:S(2)}) copy-start(bf16[12,768]{1,0:T(8,128)(2,1)} %param.5) | copy-start | bytes 55300
  98.0 21.5 %copy-start.3 = (f32[768]{0:T(1024)S(1)}, f32[768]{0:T(1024)}, u32[]{:S(2)}) copy-start(f32[768]{0:T(1024)} %param.9) | copy-start | bytes 9220

commit v4 on v3

--- a/solution.py
+++ b/solution.py
@@ -21,7 +21,7 @@
 
 
 FIRST = 10
-PLANE = [[(k + FIRST) % 16 * 2 + c for k in range(16)] for c in range(2)]
+PLANE = [[((k + FIRST) % 4 * 4 + (k + FIRST) // 4 % 4) * 2 + c for k in range(16)] for c in range(2)]
 
 
 def in_plane(members):

time: 121 us -> 120 us (level)
  the two profiles are of different devices: /device:TPU:56 before, /device:TPU:62 now
where the time goes in v4:
time: 120 us
  blocking collectives  42 us (35%)
  starting transfers between devices  36.2 us (30%)
  waiting for transfers between devices  31.5 us (26%)
  other arithmetic  5.84 us (5%)
  matrix products  2.52 us (2%)
  local copies, waits for them, and re-layouts  1.66 us (1%)
    all_gather x1, blocking collectives, on_device(): held = lax.all_gather(activated, 'q', axis=0, tiled=True)  16.8 us
    all_to_all x1, blocking collectives, in_plane(): return lax.all_to_all(members, COL, 0, 0, axis_index_groups=PLANE)  14.7 us
    all_to_all x1, waiting for transfers between devices, in_plane(): return lax.all_to_all(members, COL, 0, 0, axis_index_groups=PLANE)  13 us
    all_to_all x1, waiting for transfers between devices, on_device(): parts_up = lax.all_to_all(pair_sum.reshape(4, 4 * own, -1), 'q', 0, 0)  12.1 us
    ppermute x3, starting transfers between devices, swap(): return lax.ppermute(value, axis, [(0, 1), (1, 0)])  11.2 us
    all_gather x1, blocking collectives, on_device(): halves = lax.all_gather(summed_z.astype(bf16), 'h', axis=0)  10.5 us
    all_to_all x1, starting transfers between devices, on_device(): parts_up = lax.all_to_all(pair_sum.reshape(4, 4 * own, -1), 'q', 0, 0)  9.71 us
    ppermute x2, starting transfers between devices, trade(): return lax.ppermute(value, ('q', 'p', 'c'), pairs)  9.57 us
  transfers between devices with their start and end apart: 7, of which 4 were waited for; matrix products, arithmetic and copies ran while one was open for 5% of the time, Pallas kernels for 0%

profile of v4, /device:TPU:62, one launch (start us, length us, event | category | flops | bytes accessed | tf_op | source)
XLA Modules:
  0.0 119.8 jit_solution(10524277190036656106)
XLA Ops:
  0.0 1.9 %collective-permute-start = (bf16[768,1536]{1,0:T(8,128)(2,1)}, bf16[768,1536]{1,0:T(8,128)(2,1)S(1)}, u32[]{:S(2)}, u32[]{:S(2)}) collective-permute-start(bf16[768,1536]{1,0:T(8,128)(2,1)} %param.6), channel_id=1, source_target_pairs={{0,1},{1,0},{2,3},{3,2},{4,5},{5,4},{6,7},{7,6},{8,9},{9,8},{10,11... | collective-permute-start | bytes 7077896 | tf_op jit(solution)/shard_map/ppermute | solution.py:12
  1.9 1.5 %broadcast_in_dim.2 = bf16[16,12,768]{2,1,0:T(8,128)(2,1)} broadcast(bf16[12,768]{1,0:T(8,128)(2,1)} %param.5), dimensions={1,2} | broadcast | bytes 313344 | tf_op jit(solution)/shard_map/broadcast_in_dim | solution.py:45
  3.4 5.7 %all-to-all-start = ((bf16[16,12,768]{2,1,0:T(8,128)(2,1)}), bf16[16,12,768]{2,1,0:T(8,128)(2,1)S(1)}, u32[]{:S(2)}, u32[]{:S(2)}) async-start(bf16[16,12,768]{2,1,0:T(8,128)(2,1)} %broadcast_in_dim.2), calls=%async_computation | async-start | bytes 786432 | tf_op jit(solution)/shard_map/all_to_all | solution.py:28
  9.1 13.0 %all-to-all-done = bf16[16,12,768]{2,1,0:T(8,128)(2,1)S(1)} async-done(((bf16[16,12,768]{2,1,0:T(8,128)(2,1)}), bf16[16,12,768]{2,1,0:T(8,128)(2,1)S(1)}, u32[]{:S(2)}, u32[]{:S(2)}) %all-to-all-start) | async-done | bytes 294944 | tf_op jit(solution)/shard_map/all_to_all | solution.py:28
  22.1 0.1 reshape.23
  22.2 0.0 collective-permute-done
  22.2 2.0 %broadcast_select_fusion.2 = (bf16[768,1536]{1,0:T(8,128)(2,1)S(1)}, bf16[768,1536]{1,0:T(8,128)(2,1)S(1)}) fusion(bf16[768,1536]{1,0:T(8,128)(2,1)S(1)} %collective-permute-done, bf16[768,1536]{1,0:T(8,128)(2,1)} %param.6, pred[]{:T(512)S(6)} %eq.6), kind=kLoop, calls=%fused_computation.5 | loop fusion | flops 2359296 | bytes 9437185 | tf_op jit(solution)/shard_map/jit(_where)/select_n | solution.py:43
  24.1 0.0 copy-start
  24.2 0.6 fusion
  24.8 4.4 %collective-permute-start.1 = (bf16[192,1536]{1,0:T(8,128)(2,1)S(1)}, bf16[192,1536]{1,0:T(8,128)(2,1)S(1)}, u32[]{:S(2)}, u32[]{:S(2)}) collective-permute-start(bf16[192,1536]{1,0:T(8,128)(2,1)S(1)} %fusion), channel_id=1, source_target_pairs={{0,64},{1,449},{64,0},{65,129},{128,192},{129,65},{192,128},{193,2... | collective-permute-start | bytes 1769480 | tf_op jit(solution)/shard_map/ppermute | solution.py:20
  29.2 0.0 copy-done
  29.2 7.4 %collective-permute-start.3 = (bf16[1536,768]{1,0:T(8,128)(2,1)S(1)}, bf16[1536,768]{1,0:T(8,128)(2,1)}, u32[]{:S(2)}, u32[]{:S(2)}) collective-permute-start(bf16[1536,768]{1,0:T(8,128)(2,1)S(1)} %copy-done), channel_id=1, source_target_pairs={{0,1},{1,0},{2,3},{3,2},{4,5},{5,4},{6,7},{7,6},{8,9},{9,8},{10,11... | collective-permute-start | bytes 7077896 | tf_op jit(solution)/shard_map/ppermute | solution.py:12
  36.6 0.6 convolution_bitcast_fusion
  37.3 0.0 copy-start.2
  37.3 0.0 collective-permute-done.1
  37.3 0.9 add_convert_fusion
  38.2 9.7 %all-to-all-start.1 = ((bf16[4,48,1536]{2,1,0:T(8,128)(2,1)}), bf16[4,48,1536]{2,1,0:T(8,128)(2,1)S(1)}, u32[]{:S(2)}, u32[]{:S(2)}) async-start(bf16[4,48,1536]{2,1,0:T(8,128)(2,1)} %bitcast.2), calls=%async_computation.1 | async-start | bytes 1179648 | tf_op jit(solution)/shard_map/all_to_all | solution.py:54
  47.9 0.0 copy-done.2
  47.9 1.9 %collective-permute-start.2 = (f32[1536]{0:T(1024)S(1)}, f32[1536]{0:T(1024)S(1)}, u32[]{:S(2)}, u32[]{:S(2)}) collective-permute-start(f32[1536]{0:T(1024)S(1)} %copy-done.2), channel_id=1, source_target_pairs={{0,1},{1,0},{2,3},{3,2},{4,5},{5,4},{6,7},{7,6},{8,9},{9,8},{10,11... | collective-permute-start | bytes 18440 | tf_op jit(solution)/shard_map/ppermute | solution.py:12
  49.9 1.1 collective-permute-done.2
  51.0 12.1 %all-to-all-done.1 = bf16[4,48,1536]{2,1,0:T(8,128)(2,1)S(1)} async-done(((bf16[4,48,1536]{2,1,0:T(8,128)(2,1)}), bf16[4,48,1536]{2,1,0:T(8,128)(2,1)S(1)}, u32[]{:S(2)}, u32[]{:S(2)}) %all-to-all-start.1) | async-done | bytes 589856 | tf_op jit(solution)/shard_map/all_to_all | solution.py:54
  63.1 0.1 convert_reduce_fusion
  63.2 10.5 %all-gather = bf16[96,1536]{1,0:T(8,128)(2,1)S(1)} all-gather(bf16[48,1536]{1,0:T(8,128)(2,1)S(1)} %convert_element_type.55), channel_id=2, replica_groups=mesh['q'=4,'p'=2,'h'=2,'x'=4,'y'=4,'c'=2] {'h'}, dimensions={0}, use_global_device_ids=true | all-gather | bytes 442368 | tf_op jit(solution)/shard_map/all_gather | solution.py:56
  73.8 0.1 fusion.9
  73.9 16.8 %all_gather.8 = bf16[192,1536]{1,0:T(8,128)(2,1)S(1)} all-gather(bf16[48,1536]{1,0:T(8,128)(2,1)S(1)} %fusion.9), channel_id=1, replica_groups=mesh['q'=4,'p'=2,'h'=2,'x'=4,'y'=4,'c'=2] {'q'}, dimensions={0}, use_global_device_ids=true | all-gather | bytes 737280 | tf_op jit(solution)/shard_map/all_gather | solution.py:60
  90.7 5.2 %collective-permute-start.4 = (bf16[192,1536]{1,0:T(8,128)(2,1)S(1)}, bf16[192,1536]{1,0:T(8,128)(2,1)S(1)}, u32[]{:S(2)}, u32[]{:S(2)}) collective-permute-start(bf16[192,1536]{1,0:T(8,128)(2,1)S(1)} %all_gather.8), channel_id=1, source_target_pairs={{0,64},{1,449},{64,0},{65,129},{128,192},{129,65},{192,128},{193,2... | collective-permute-start | bytes 1769480 | tf_op jit(solution)/shard_map/ppermute | solution.py:20
  95.9 0.0 collective-permute-done.3
  95.9 2.0 %broadcast_select_fusion = (bf16[1536,768]{1,0:T(8,128)(2,1)S(1)}, bf16[1536,768]{1,0:T(8,128)(2,1)S(1)}) fusion(bf16[1536,768]{1,0:T(8,128)(2,1)} %collective-permute-done.3, bf16[1536,768]{1,0:T(8,128)(2,1)S(1)} %copy-done, pred[]{:T(512)S(6)} %eq.6), kind=kLoop, calls=%fused_computation.3 | loop fusion | flops 2359296 | bytes 9437185 | tf_op jit(solution)/shard_map/jit(_where)/select_n | solution.py:43
  97.9 0.6 fusion.11
  98.5 0.0 copy-start.1
  98.5 0.0 copy-start.3
  98.5 5.2 %collective-permute-done.4 = bf16[192,1536]{1,0:T(8,128)(2,1)S(1)} collective-permute-done((bf16[192,1536]{1,0:T(8,128)(2,1)S(1)}, bf16[192,1536]{1,0:T(8,128)(2,1)S(1)}, u32[]{:S(2)}, u32[]{:S(2)}) %collective-permute-start.4) | collective-permute-done | bytes 589856 | tf_op jit(solution)/shard_map/ppermute | solution.py:20
  103.7 0.6 fusion.1
  104.4 0.1 reshape.25
  104.5 14.7 %all_to_all.15 = bf16[16,12,768]{2,1,0:T(8,128)(2,1)S(1)} all-to-all(bf16[16,12,768]{2,1,0:T(8,128)(2,1)S(1)} %reshape.25), channel_id=1, replica_groups={{20,28,6,14,22,30,0,8,16,24,2,10,18,26,4,12},{21,29,7,15,23,31,1,9,17,2..., dimensions={0} | all-to-all | bytes 589824 | tf_op jit(solution)/shard_map/all_to_all | solution.py:28
  119.1 0.1 convert_reduce_fusion.1
  119.2 0.0 copy-done.1
  119.2 0.0 copy-done.3
  119.2 0.6 add_convert_fusion.1
  (2 shorter events, 0.0 us)
Async XLA Ops:
  0.0 22.2 %collective-permute-start = (bf16[768,1536]{1,0:T(8,128)(2,1)}, bf16[768,1536]{1,0:T(8,128)(2,1)S(1)}, u32[]{:S(2)}, u32[]{:S(2)}) collective-permute-start(bf16[768,1536]{1,0:T(8,128)(2,1)} %param.6), channel_id=1, source_target_pairs={{0,1},{1,0},{2,3},{3,2},{4,5},{5,4},{6,7},{7,6},{8,9},{9,8},{10,11... | collective-permute-start | bytes 7077896 | tf_op jit(solution)/shard_map/ppermute | solution.py:12
  3.4 18.7 %all-to-all-start = ((bf16[16,12,768]{2,1,0:T(8,128)(2,1)}), bf16[16,12,768]{2,1,0:T(8,128)(2,1)S(1)}, u32[]{:S(2)}, u32[]{:S(2)}) async-start(bf16[16,12,768]{2,1,0:T(8,128)(2,1)} %broadcast_in_dim.2), calls=%async_computation | async-start | bytes 786432 | tf_op jit(solution)/shard_map/all_to_all | solution.py:28
  24.1 5.1 %copy-start = (bf16[1536,768]{1,0:T(8,128)(2,1)S(1)}, bf16[1536,768]{1,0:T(8,128)(2,1)}, u32[]{:S(2)}) copy-start(bf16[1536,768]{1,0:T(8,128)(2,1)} %param.8) | copy-start | bytes 7077892
  24.8 12.5 %collective-permute-start.1 = (bf16[192,1536]{1,0:T(8,128)(2,1)S(1)}, bf16[192,1536]{1,0:T(8,128)(2,1)S(1)}, u32[]{:S(2)}, u32[]{:S(2)}) collective-permute-start(bf16[192,1536]{1,0:T(8,128)(2,1)S(1)} %fusion), channel_id=1, source_target_pairs={{0,64},{1,449},{64,0},{65,129},{128,192},{129,65},{192,128},{193,2... | collective-permute-start | bytes 1769480 | tf_op jit(solution)/shard_map/ppermute | solution.py:20
  29.2 66.7 %collective-permute-start.3 = (bf16[1536,768]{1,0:T(8,128)(2,1)S(1)}, bf16[1536,768]{1,0:T(8,128)(2,1)}, u32[]{:S(2)}, u32[]{:S(2)}) collective-permute-start(bf16[1536,768]{1,0:T(8,128)(2,1)S(1)} %copy-done), channel_id=1, source_target_pairs={{0,1},{1,0},{2,3},{3,2},{4,5},{5,4},{6,7},{7,6},{8,9},{9,8},{10,11... | collective-permute-start | bytes 7077896 | tf_op jit(solution)/shard_map/ppermute | solution.py:12
  37.3 10.7 %copy-start.2 = (f32[1536]{0:T(1024)S(1)}, f32[1536]{0:T(1024)}, u32[]{:S(2)}) copy-start(f32[1536]{0:T(1024)} %param.7) | copy-start | bytes 18436
  38.2 24.9 %all-to-all-start.1 = ((bf16[4,48,1536]{2,1,0:T(8,128)(2,1)}), bf16[4,48,1536]{2,1,0:T(8,128)(2,1)S(1)}, u32[]{:S(2)}, u32[]{:S(2)}) async-start(bf16[4,48,1536]{2,1,0:T(8,128)(2,1)} %bitcast.2), calls=%async_computation.1 | async-start | bytes 1179648 | tf_op jit(solution)/shard_map/all_to_all | solution.py:54
  47.9 3.1 %collective-permute-start.2 = (f32[1536]{0:T(1024)S(1)}, f32[1536]{0:T(1024)S(1)}, u32[]{:S(2)}, u32[]{:S(2)}) collective-permute-start(f32[1536]{0:T(1024)S(1)} %copy-done.2), channel_id=1, source_target_pairs={{0,1},{1,0},{2,3},{3,2},{4,5},{5,4},{6,7},{7,6},{8,9},{9,8},{10,11... | collective-permute-start | bytes 18440 | tf_op jit(solution)/shard_map/ppermute | solution.py:12
  90.7 13.0 %collective-permute-start.4 = (bf16[192,1536]{1,0:T(8,128)(2,1)S(1)}, bf16[192,1536]{1,0:T(8,128)(2,1)S(1)}, u32[]{:S(2)}, u32[]{:S(2)}) collective-permute-start(bf16[192,1536]{1,0:T(8,128)(2,1)S(1)} %all_gather.8), channel_id=1, source_target_pairs={{0,64},{1,449},{64,0},{65,129},{128,192},{129,65},{192,128},{193,2... | collective-permute-start | bytes 1769480 | tf_op jit(solution)/shard_map/ppermute | solution.py:20
  98.5 20.7 %copy-start.1 = (bf16[12,768]{1,0:T(8,128)(2,1)S(1)}, bf16[12,768]{1,0:T(8,128)(2,1)}, u32[]{:S(2)}) copy-start(bf16[12,768]{1,0:T(8,128)(2,1)} %param.5) | copy-start | bytes 55300
  98.5 20.7 %copy-start.3 = (f32[768]{0:T(1024)S(1)}, f32[768]{0:T(1024)}, u32[]{:S(2)}) copy-start(f32[768]{0:T(1024)} %param.9) | copy-start | bytes 9220
